TPU v7x, 256 devices: a whole 4x4x8 slice. The times are simulated.
256 devices in a mesh: station: 64 (over x, z, core), sample: 4 (over y).
Axes of the slice: x: 4, y: 4, z: 8, core: 2. Of those that a mesh axis runs over, the one named last changes fastest.
Arguments:
- flux: bfloat16 [16, 2048, 3584], P('sample', 'station'), may hold values from -6 to 6
- coeff: float32 [2048, 3584], P('station'), may hold values from 0.02 to 0.24
- diff_steps: int32 [16], P('sample'), may hold values from 3 to 6, as said below
- footprint: bfloat16 [1024, 4, 16384], P('station'), may hold values from -0.03125 to 0.03125
- tile_src: int32 [1024, 4, 1], replicated, may hold values from 0 to 63; in each aligned block of 64 rows (0 to 63, 64 to 127, ..., all dimensions but the last counted through in order) at most 2 rows name the same one
- tile_local: int32 [1024, 4], replicated, may hold values from 0 to 6
- tile_count: int32 [1024], P('station'), may hold values from 1 to 4
Outputs:
- observed: float32 [1024, 16], P('station')
Inputs may be any that keep to these rules, and one draw needn't show every extreme that they name: `tile_src`: in each aligned block of 64 rows (the slots of one index's stations, stations and slots in order), no band appears more than 2 times, and some band appears exactly 2 times. `diff_steps`: some sample takes 6 steps and another takes 3.
All inputs are finite; a program needn't handle non-finite values.
Results may differ from a plain program's by a relative error of at most 0.0029.
Values may be sent and summed in bfloat16 or wider, within the bound.
No kernel may reach another device: no remote copies, remote signals or barrier semaphores. Data moves between devices by JAX's collectives and lax.ppermute only.
A program may use at most 128 MiB of HBM per device.

v0:
```python
import jax
import jax.numpy as jnp
from jax import lax
from jax.sharding import PartitionSpec as P

TILE_LON = 512
TILES_DEV = 7
KT = 4
ITERS = 6


def extended_2(cells, sides, width):
    for axis, dim in sides:
        count = lax.axis_size(axis)
        ends = count - 1
        head = lax.slice_in_dim(cells, 0, width, axis=dim)
        tail = lax.slice_in_dim(cells, cells.shape[dim] - width, cells.shape[dim], axis=dim)
        cells = jnp.concatenate(
            [
                lax.ppermute(tail, axis, [(i, (i + 1) % count) for i in range(ends)]),
                cells,
                lax.ppermute(head, axis, [((i + 1) % count, i) for i in range(ends)]),
            ],
            axis=dim,
        )
    return cells


def diffuse_rows(extended, gates):
    field = extended[:-1]
    coefs = extended[-1]
    center = field[:, 1:-1]
    lap = (
        field[:, :-2]
        + field[:, 2:]
        + jnp.roll(center, 1, 2)
        + jnp.roll(center, -1, 2)
        - 4.0 * center
    )
    update = gates[:, None, None] * coefs[None, 1:-1] * lap
    return (center + update, coefs[1:-1])


def body(flux, coeff, diff_steps, footprint, tile_src, tile_local, tile_count):
    samples_here, rows_here, lon_count = flux.shape
    stations_here = footprint.shape[0]
    devices = lax.axis_size("station")
    own_index = lax.axis_index("station")
    cap_slots = 2 * max(1, (stations_here * KT + devices - 1) // devices)
    field = flux.astype(jnp.float32)
    for step_index in range(ITERS):
        gates = (step_index < diff_steps).astype(jnp.float32)
        stacked = jnp.concatenate([field, coeff[None]], axis=0)
        extended = extended_2(stacked, (("station", 1),), 1)
        field, unused = diffuse_rows(extended, gates)
    final = field.astype(jnp.bfloat16)
    tiles = final.reshape(samples_here, rows_here, TILES_DEV, TILE_LON)
    tiles = tiles.transpose(2, 0, 1, 3).reshape(TILES_DEV, samples_here, rows_here * TILE_LON)
    slot_count = stations_here * KT
    order = jnp.arange(slot_count, dtype=jnp.int32)
    src_all = tile_src[:, :, 0].reshape(devices, slot_count)
    loc_all = tile_local.reshape(devices, slot_count)
    earlier = order[None, :] < order[:, None]
    same_src = src_all[:, :, None] == src_all[:, None, :]
    rank_all = jnp.sum((same_src & earlier[None]).astype(jnp.int32), axis=2)
    cap_range = jnp.arange(cap_slots, dtype=jnp.int32)
    band_range = jnp.arange(devices, dtype=jnp.int32)
    my_src = lax.dynamic_index_in_dim(src_all, own_index, 0, keepdims=False)
    my_rank = lax.dynamic_index_in_dim(rank_all, own_index, 0, keepdims=False)
    pick = (my_src[None, None, :] == band_range[:, None, None]) & (
        my_rank[None, None, :] == cap_range[None, :, None]
    )
    slot_of = jnp.sum(jnp.where(pick, order[None, None, :], 0), axis=2)
    has_slot = jnp.any(pick, axis=2)
    prints_flat = footprint.reshape(slot_count, footprint.shape[2])
    prints_laid = jnp.where(has_slot[:, :, None], prints_flat[slot_of], jnp.zeros((), jnp.bfloat16))
    chosen = (src_all[:, None, :] == own_index) & (rank_all[:, None, :] == cap_range[None, :, None])
    send_loc = jnp.sum(jnp.where(chosen, loc_all[:, None, :], 0), axis=2)
    filled = jnp.any(chosen, axis=2)
    outgoing = jnp.where(filled[:, :, None, None], tiles[send_loc], jnp.zeros((), jnp.bfloat16))
    arrived = lax.all_to_all(outgoing, "station", split_axis=0, concat_axis=0, tiled=True)
    slot_value = jnp.einsum(
        "ncst,nct->ncs", arrived, prints_laid, preferred_element_type=jnp.float32
    )
    live = (order % KT < tile_count[order // KT]).astype(jnp.float32)
    assign = pick.astype(jnp.float32) * live[None, None, :]
    station_hot = (
        (order // KT)[None, :] == jnp.arange(stations_here, dtype=jnp.int32)[:, None]
    ).astype(jnp.float32)
    weights = jnp.einsum("aj,dcj->adc", station_hot, assign, precision=lax.Precision.HIGHEST)
    observed = jnp.dot(
        weights.reshape(stations_here, devices * cap_slots),
        slot_value.reshape(devices * cap_slots, samples_here),
        precision=lax.Precision.HIGHEST,
        preferred_element_type=jnp.float32,
    )
    return lax.all_gather(observed, "sample", axis=1, tiled=True)


def solution(mesh):
    in_specs = (
        P("sample", "station", None),
        P("station", None),
        P("sample"),
        P("station", None, None),
        P(),
        P(),
        P("station"),
    )
    out_specs = P("station", None)
    return jax.shard_map(body, mesh=mesh, in_specs=in_specs, out_specs=out_specs, check_vma=False)
```

profile of v0, /device:TPU:8, one launch (start us, length us, event | category | flops | bytes accessed | tf_op | source)
XLA Modules:
  0.0 549.9 jit_solution(17744105900552351858)
XLA Ops:
  0.0 1.9 copy_convert_fusion
  2.0 0.5 copy.58
  2.4 0.7 fusion.57
  3.2 1.3 collective-permute-start.1
  4.5 3.7 collective-permute-start
  8.2 2.8 fusion.82
  11.0 0.7 fusion.83
  11.8 0.2 copy.55
  12.0 0.3 reshape_squeeze.3
  12.3 1.2 compare_convert_fusion
  13.5 0.9 copy.66
  14.4 0.8 broadcast_in_dim.44
  15.3 1.8 convert_reduce_fusion
  17.2 0.1 fusion.61
  17.3 0.9 select_reduce_fusion
  18.3 0.1 reshape.220
  18.4 0.1 copy.56
  18.5 5.5 %fusion.9 = f32[4,32,3584]{2,0,1:T(4,128)S(1)} fusion(f32[4,32,3584]{2,0,1:T(4,128)S(1)} %copy_convert_fusion, f32[1,32,3584]{2,0,1:T(1,128)S(1)} %copy.58, f32[5,1,3584]{2,0,1:T(8,128)} %collective-permute-done.1, f32[5,1,3584]{2,0,1:T(8,128)} %collective-permute-done, f32[4,32,3583]{2,0,1:T(4,128)} %get-tuple-element.40, ...), kind=kLoop, calls=%fused_computation.34 | loop fusion | flops 6422528 | bytes 8400912 | tf_op jit(solution)/shard_map/add | solution.py:41
  24.1 1.1 fusion.80
  25.2 1.3 collective-permute-start.3
  26.5 3.4 collective-permute-start.2
  30.1 0.8 collective-permute-done.2
  30.9 4.7 fusion.16
  35.7 1.1 fusion.78
  36.7 1.3 collective-permute-start.5
  38.0 5.3 collective-permute-start.4
  43.4 0.7 collective-permute-done.4
  44.1 4.7 fusion.23
  48.8 1.1 fusion.76
  49.9 1.3 collective-permute-start.7
  51.2 5.8 %collective-permute-start.6 = (f32[5,1,3584]{2,0,1:T(8,128)S(1)}, f32[5,1,3584]{2,0,1:T(8,128)S(1)}, u32[]{:S(2)}, u32[]{:S(2)}) collective-permute-start(f32[5,1,3584]{2,0,1:T(8,128)S(1)} %get-tuple-element.25), channel_id=1, source_target_pairs={{0,4},{4,8},{8,12},{12,16},{16,20},{20,24},{24,28},{28,32},{32,36}... | collective-permute-start | bytes 215048 | tf_op jit(solution)/shard_map/ppermute | solution.py:20
  57.1 0.8 collective-permute-done.6
  58.0 4.7 fusion.30
  62.7 1.1 fusion.74
  63.8 1.3 collective-permute-start.9
  65.1 5.8 %collective-permute-start.8 = (f32[5,1,3584]{2,0,1:T(8,128)S(1)}, f32[5,1,3584]{2,0,1:T(8,128)S(1)}, u32[]{:S(2)}, u32[]{:S(2)}) collective-permute-start(f32[5,1,3584]{2,0,1:T(8,128)S(1)} %get-tuple-element.19), channel_id=1, source_target_pairs={{0,4},{4,8},{8,12},{12,16},{16,20},{20,24},{24,28},{28,32},{32,36}... | collective-permute-start | bytes 215048 | tf_op jit(solution)/shard_map/ppermute | solution.py:20
  71.0 0.8 collective-permute-done.8
  71.8 4.7 fusion.37
  76.5 1.1 fusion.73
  77.6 1.3 collective-permute-start.11
  78.9 6.0 %collective-permute-start.10 = (f32[5,1,3584]{2,0,1:T(8,128)S(1)}, f32[5,1,3584]{2,0,1:T(8,128)S(1)}, u32[]{:S(2)}, u32[]{:S(2)}) collective-permute-start(f32[5,1,3584]{2,0,1:T(8,128)S(1)} %get-tuple-element.9), channel_id=1, source_target_pairs={{0,4},{4,8},{8,12},{12,16},{16,20},{20,24},{24,28},{28,32},{32,36}... | collective-permute-start | bytes 215048 | tf_op jit(solution)/shard_map/ppermute | solution.py:20
  85.1 0.6 collective-permute-done.10
  85.7 4.7 fusion.51
  90.4 0.6 reshape.242
  91.0 0.6 copy.65
  91.6 0.7 reshape.208
  92.3 17.1 %gather_fusion.1 = bf16[128,4,16384]{2,1,0:T(4,128)(2,1)} fusion(bf16[7,4,16384]{2,1,0:T(4,128)(2,1)S(1)} %reshape.208, s32[1024]{0:T(1024)S(1)} %pad_clamp_fusion.2), kind=kCustom, calls=%fused_computation.1 | custom fusion | bytes 33554944 | tf_op jit(solution)/shard_map/gather | solution.py:80
  109.4 12.1 %broadcast_select_fusion = bf16[64,2,4,16384]{3,2,1,0:T(4,128)(2,1)} fusion(bf16[64,2,4,16384]{3,2,1,0:T(4,128)(2,1)} %bitcast.39, pred[64,2]{1,0:T(8,128)(4,1)S(1)} %copy.56), kind=kLoop, calls=%fused_computation.3 | loop fusion | flops 8388608 | bytes 33554560 | tf_op jit(solution)/shard_map/jit(_where)/select_n | solution.py:80
  121.5 26.9 %all-to-all-start = ((bf16[64,2,4,16384]{3,2,1,0:T(4,128)(2,1)}), bf16[64,2,4,16384]{3,2,1,0:T(4,128)(2,1)}, u32[]{:S(2)}, u32[]{:S(2)}) async-start(bf16[64,2,4,16384]{3,2,1,0:T(4,128)(2,1)} %broadcast_select_fusion), calls=%async_computation | async-start | bytes 33554432 | tf_op jit(solution)/shard_map/all_to_all | solution.py:81
  148.4 2.6 reshape.209
  151.0 0.1 fusion.59
  151.2 0.1 reshape.228
  151.4 5.3 gather_fusion.2
  156.7 7.6 %reshape.227 = bf16[64,2,16384]{2,1,0:T(2,128)(2,1)} reshape(bf16[128,16384]{1,0:T(8,128)(2,1)} %gather_fusion.2) | data formatting | bytes 8388608 | tf_op jit(solution)/shard_map/gather | solution.py:76
  164.3 0.1 and_reduce_fusion
  164.4 0.1 copy.68
  164.6 0.8 gather_fusion
  165.4 0.2 fusion.58
  165.5 7.7 %fusion.2 = bf16[64,2,16384,1]{2,1,0,3:T(2,128)(2,1)} fusion(bf16[64,2,16384]{2,1,0:T(2,128)(2,1)} %reshape.227, pred[64,2]{1,0:T(8,128)(4,1)S(1)} %copy.68), kind=kLoop, calls=%fused_computation.7 | loop fusion | flops 2097152 | bytes 8388736 | tf_op jit(solution)/shard_map/jit(_where)/select_n | solution.py:76
  173.2 339.5 %all-to-all-done = bf16[64,2,4,16384]{3,2,1,0:T(4,128)(2,1)} async-done(((bf16[64,2,4,16384]{3,2,1,0:T(4,128)(2,1)}), bf16[64,2,4,16384]{3,2,1,0:T(4,128)(2,1)}, u32[]{:S(2)}, u32[]{:S(2)}) %all-to-all-start) | async-done | bytes 16777248 | tf_op jit(solution)/shard_map/all_to_all | solution.py:81
  512.7 25.3 %fusion = f32[64,2,1,4]{3,2,1,0:T(1,128)S(1)} fusion(bf16[64,2,4,16384]{3,2,1,0:T(4,128)(2,1)} %all-to-all-done, bf16[64,2,16384,1]{2,1,0,3:T(2,128)(2,1)} %fusion.2), kind=kOutput, calls=%fused_computation.5 | convolution fusion | flops 16777216 | bytes 20973568 | tf_op jit(solution)/shard_map/ncst,nct->ncs/dot_general | solution.py:82
  538.1 0.1 convolution_bitcast_fusion
  538.3 11.0 %all-gather = f32[4,4,16]{2,1,0:T(4,128)S(1)} all-gather(f32[1,4,16]{2,1,0:T(4,128)S(1)} %convolution_bitcast_fusion), channel_id=1, replica_groups=mesh['station'=64,'sample'=4] {'sample'}, dimensions={0}, use_global_device_ids=true | all-gather | bytes 1280 | tf_op jit(solution)/shard_map/all_gather | solution.py:97
  549.2 0.7 copy.70
  (47 shorter events, 1.1 us)
Async XLA Ops:
  0.0 164.6 %copy-start = (s32[16]{0:T(128)S(1)}, s32[16]{0:T(128)}, u32[]{:S(2)}) copy-start(s32[16]{0:T(128)} %param.13) | copy-start | bytes 196
  0.0 1.9 copy-start.1
  3.2 15.3 %collective-permute-start.1 = (f32[5,1,3584]{2,0,1:T(8,128)}, f32[5,1,3584]{2,0,1:T(8,128)}, u32[]{:S(2)}, u32[]{:S(2)}) collective-permute-start(f32[5,1,3584]{2,0,1:T(8,128)} %get-tuple-element.43), channel_id=1, source_target_pairs={{4,0},{8,4},{12,8},{16,12},{20,16},{24,20},{28,24},{32,28},{36,32}... | collective-permute-start | bytes 215048 | tf_op jit(solution)/shard_map/ppermute | solution.py:22
  4.5 14.1 %collective-permute-start = (f32[5,1,3584]{2,0,1:T(8,128)}, f32[5,1,3584]{2,0,1:T(8,128)}, u32[]{:S(2)}, u32[]{:S(2)}) collective-permute-start(f32[5,1,3584]{2,0,1:T(8,128)} %get-tuple-element.5), channel_id=1, source_target_pairs={{0,4},{4,8},{8,12},{12,16},{16,20},{20,24},{24,28},{28,32},{32,36}... | collective-permute-start | bytes 215048 | tf_op jit(solution)/shard_map/ppermute | solution.py:20
  8.2 3.6 copy-start.2
  25.2 5.7 %copy-start.6 = (f32[4]{0:T(128)S(1)}, f32[4]{0:T(128)}, u32[]{:S(2)}) copy-start(f32[4]{0:T(128)} %get-tuple-element.48) | copy-start | bytes 52
  25.2 4.8 collective-permute-start.3
  26.5 4.4 collective-permute-start.2
  35.6 8.4 %copy-start.5 = (f32[4]{0:T(128)S(1)}, f32[4]{0:T(128)}, u32[]{:S(2)}) copy-start(f32[4]{0:T(128)} %get-tuple-element.47) | copy-start | bytes 52
  36.7 6.7 %collective-permute-start.5 = (f32[5,1,3584]{2,0,1:T(8,128)S(1)}, f32[5,1,3584]{2,0,1:T(8,128)S(1)}, u32[]{:S(2)}, u32[]{:S(2)}) collective-permute-start(f32[5,1,3584]{2,0,1:T(8,128)S(1)} %get-tuple-element.32), channel_id=1, source_target_pairs={{4,0},{8,4},{12,8},{16,12},{20,16},{24,20},{28,24},{32,28},{36,32}... | collective-permute-start | bytes 215048 | tf_op jit(solution)/shard_map/ppermute | solution.py:22
  38.0 6.1 %collective-permute-start.4 = (f32[5,1,3584]{2,0,1:T(8,128)S(1)}, f32[5,1,3584]{2,0,1:T(8,128)S(1)}, u32[]{:S(2)}, u32[]{:S(2)}) collective-permute-start(f32[5,1,3584]{2,0,1:T(8,128)S(1)} %get-tuple-element.31), channel_id=1, source_target_pairs={{0,4},{4,8},{8,12},{12,16},{16,20},{20,24},{24,28},{28,32},{32,36}... | collective-permute-start | bytes 215048 | tf_op jit(solution)/shard_map/ppermute | solution.py:20
  48.8 9.1 %copy-start.4 = (f32[4]{0:T(128)S(1)}, f32[4]{0:T(128)}, u32[]{:S(2)}) copy-start(f32[4]{0:T(128)} %get-tuple-element.46) | copy-start | bytes 52
  49.9 7.2 %collective-permute-start.7 = (f32[5,1,3584]{2,0,1:T(8,128)S(1)}, f32[5,1,3584]{2,0,1:T(8,128)S(1)}, u32[]{:S(2)}, u32[]{:S(2)}) collective-permute-start(f32[5,1,3584]{2,0,1:T(8,128)S(1)} %get-tuple-element.26), channel_id=1, source_target_pairs={{4,0},{8,4},{12,8},{16,12},{20,16},{24,20},{28,24},{32,28},{36,32}... | collective-permute-start | bytes 215048 | tf_op jit(solution)/shard_map/ppermute | solution.py:22
  51.2 6.7 %collective-permute-start.6 = (f32[5,1,3584]{2,0,1:T(8,128)S(1)}, f32[5,1,3584]{2,0,1:T(8,128)S(1)}, u32[]{:S(2)}, u32[]{:S(2)}) collective-permute-start(f32[5,1,3584]{2,0,1:T(8,128)S(1)} %get-tuple-element.25), channel_id=1, source_target_pairs={{0,4},{4,8},{8,12},{12,16},{16,20},{20,24},{24,28},{28,32},{32,36}... | collective-permute-start | bytes 215048 | tf_op jit(solution)/shard_map/ppermute | solution.py:20
  62.7 9.1 %copy-start.3 = (f32[4]{0:T(128)S(1)}, f32[4]{0:T(128)}, u32[]{:S(2)}) copy-start(f32[4]{0:T(128)} %get-tuple-element.50) | copy-start | bytes 52
  63.8 7.2 %collective-permute-start.9 = (f32[5,1,3584]{2,0,1:T(8,128)S(1)}, f32[5,1,3584]{2,0,1:T(8,128)S(1)}, u32[]{:S(2)}, u32[]{:S(2)}) collective-permute-start(f32[5,1,3584]{2,0,1:T(8,128)S(1)} %get-tuple-element.20), channel_id=1, source_target_pairs={{4,0},{8,4},{12,8},{16,12},{20,16},{24,20},{28,24},{32,28},{36,32}... | collective-permute-start | bytes 215048 | tf_op jit(solution)/shard_map/ppermute | solution.py:22
  65.1 6.7 %collective-permute-start.8 = (f32[5,1,3584]{2,0,1:T(8,128)S(1)}, f32[5,1,3584]{2,0,1:T(8,128)S(1)}, u32[]{:S(2)}, u32[]{:S(2)}) collective-permute-start(f32[5,1,3584]{2,0,1:T(8,128)S(1)} %get-tuple-element.19), channel_id=1, source_target_pairs={{0,4},{4,8},{8,12},{12,16},{16,20},{20,24},{24,28},{28,32},{32,36}... | collective-permute-start | bytes 215048 | tf_op jit(solution)/shard_map/ppermute | solution.py:20
  77.6 7.4 %collective-permute-start.11 = (f32[5,1,3584]{2,0,1:T(8,128)S(1)}, f32[5,1,3584]{2,0,1:T(8,128)S(1)}, u32[]{:S(2)}, u32[]{:S(2)}) collective-permute-start(f32[5,1,3584]{2,0,1:T(8,128)S(1)} %get-tuple-element.10), channel_id=1, source_target_pairs={{4,0},{8,4},{12,8},{16,12},{20,16},{24,20},{28,24},{32,28},{36,32}... | collective-permute-start | bytes 215048 | tf_op jit(solution)/shard_map/ppermute | solution.py:22
  78.9 6.7 %collective-permute-start.10 = (f32[5,1,3584]{2,0,1:T(8,128)S(1)}, f32[5,1,3584]{2,0,1:T(8,128)S(1)}, u32[]{:S(2)}, u32[]{:S(2)}) collective-permute-start(f32[5,1,3584]{2,0,1:T(8,128)S(1)} %get-tuple-element.9), channel_id=1, source_target_pairs={{0,4},{4,8},{8,12},{12,16},{16,20},{20,24},{24,28},{28,32},{32,36}... | collective-permute-start | bytes 215048 | tf_op jit(solution)/shard_map/ppermute | solution.py:20
  121.5 391.2 %all-to-all-start = ((bf16[64,2,4,16384]{3,2,1,0:T(4,128)(2,1)}), bf16[64,2,4,16384]{3,2,1,0:T(4,128)(2,1)}, u32[]{:S(2)}, u32[]{:S(2)}) async-start(bf16[64,2,4,16384]{3,2,1,0:T(4,128)(2,1)} %broadcast_select_fusion), calls=%async_computation | async-start | bytes 33554432 | tf_op jit(solution)/shard_map/all_to_all | solution.py:81
where the time goes:
time: 552 us; the launch traced here: 550 us
  waiting for transfers between devices  343 us (62%)
  starting transfers between devices  64.6 us (12%)
  other arithmetic  56.2 us (10%)
  local copies, waits for them, and re-layouts  48.8 us (9%)
  matrix products  25.6 us (5%)
  blocking collectives  11 us (2%)
    all_to_all x1, waiting for transfers between devices, body(): lax.all_to_all(outgoing, 'station', split_axis=0, concat_axis=0, tiled=True)  340 us
    ppermute x6, starting transfers between devices, extended_2(): lax.ppermute(tail, axis, [(i, (i + 1) % count) for i in range(ends)])  30 us
    all_to_all x1, starting transfers between devices, body(): lax.all_to_all(outgoing, 'station', split_axis=0, concat_axis=0, tiled=True)  26.9 us
    dot_general x1, matrix products, body(): jnp.einsum('ncst,nct->ncs', arrived, prints_laid, preferred_element_type=...  25.3 us
    add x5, other arithmetic, diffuse_rows(): return (center + update, coefs[1:-1])  24.3 us
    gather x1, local copies, waits for them, and re-layouts, body(): tiles[send_loc]  17.1 us
    gather x2, local copies, waits for them, and re-layouts, body(): prints_flat[slot_of]  12.9 us
    select_n x1, other arithmetic, body(): jnp.where(filled[:, :, None, None], tiles[send_loc], jnp.zeros((), jnp.bf...  12.1 us
  transfers between devices with their start and end apart: 13, of which 6 were waited for; matrix products, arithmetic and copies ran while one was open for 6% of the time, Pallas kernels for 0%

commit v1 on v0

v1 whole, which is shorter than its diff:
```python
import jax
import jax.numpy as jnp
from jax import lax
from jax.experimental import pallas as pl
from jax.experimental.pallas import tpu as pltpu
from jax.sharding import PartitionSpec as P

TILE_LON = 512
TILES_DEV = 7
KT = 4
ITERS = 6
CAP = 2
HALO = 8
PARTS = 4
VMEM = pltpu.VMEM
SMEM = pltpu.SMEM


def spec(space):
    return pl.BlockSpec(memory_space=space)


def pack_kernel(src_ref, prints_ref, sent_ref, place_ref, held_ref, slot_ref):
    slots = prints_ref.shape[0]
    bands = sent_ref.shape[0]

    def clear(i, carry):
        held_ref[i] = 0
        slot_ref[2 * i] = 0
        slot_ref[2 * i + 1] = 0
        return carry

    lax.fori_loop(0, bands, clear, 0)

    def assign(j, carry):
        band = src_ref[j]
        rank = jnp.minimum(held_ref[band], CAP - 1)
        held_ref[band] = rank + 1
        place_ref[j] = CAP * band + rank
        slot_ref[CAP * band + rank] = j
        return carry

    lax.fori_loop(0, slots, assign, 0)

    def fill(i, carry):
        first = prints_ref[slot_ref[2 * i]]
        second = prints_ref[slot_ref[2 * i + 1]]
        sent_ref[i] = jnp.concatenate([first, second], axis=0)
        return carry

    lax.fori_loop(0, bands, fill, 0, unroll=4)


def diffuse_kernel(
    own_ref, steps_ref, flux_ref, above_ref, below_ref, coef_ref, coef_above_ref, coef_below_ref,
    out_ref, field_ref, coefs_ref,
):
    own = own_ref[0]
    samples, rows, lon = flux_ref.shape
    tall = rows + 2 * HALO
    coefs_ref[0:HALO] = coef_above_ref[...]
    coefs_ref[HALO : HALO + rows] = coef_ref[...]
    coefs_ref[HALO + rows :] = coef_below_ref[...]
    edge = jnp.zeros((HALO, lon), jnp.float32)
    for pair in range(samples // 2):
        ends = []
        for side in range(2):
            sample = 2 * pair + side
            for turn in range(2):
                field_ref[side, turn, 0:HALO] = edge
                field_ref[side, turn, HALO + tall :] = edge
            field_ref[side, 0, HALO : 2 * HALO] = above_ref[sample].astype(jnp.float32)
            field_ref[side, 0, 2 * HALO : 2 * HALO + rows] = flux_ref[sample].astype(jnp.float32)
            field_ref[side, 0, 2 * HALO + rows : 3 * HALO + rows] = below_ref[sample].astype(jnp.float32)
            count = jnp.minimum(steps_ref[sample], ITERS)

            def step(k, carry, side=side):
                turn = lax.rem(k, 2)
                for tile in range(tall // 8):
                    at = HALO + 8 * tile
                    center = field_ref[side, turn, at : at + 8]
                    north = field_ref[side, turn, at - 1 : at + 7]
                    south = field_ref[side, turn, at + 1 : at + 9]
                    east = pltpu.roll(center, lon - 1, 1)
                    west = pltpu.roll(center, 1, 1)
                    lap = (north + south + east + west) - 4.0 * center
                    field_ref[side, 1 - turn, at : at + 8] = center + coefs_ref[8 * tile : 8 * tile + 8] * lap
                return carry

            lax.fori_loop(0, count, step, 0)
            ends.append(lax.rem(count, 2))
        for part in range(PARTS):
            at = 2 * HALO + 8 * part
            both = jnp.concatenate([field_ref[side, ends[side], at : at + 8] for side in range(2)], axis=0)
            out_ref[lax.rem(part + PARTS - own, PARTS), 16 * pair : 16 * pair + 16] = both.astype(jnp.bfloat16)


def dots_kernel(own_ref, loc_ref, prints_ref, own_part, part1, part2, part3, out_ref, cells_ref, sums_ref):
    own = own_ref[0]
    bands, _, width = prints_ref.shape
    slots = bands * CAP
    for turn, part in enumerate((own_part, part1, part2, part3)):
        at = pl.multiple_of(lax.rem(own + turn, PARTS) * 32, 32)
        cells_ref[pl.ds(at, 32)] = part[...]
    prints = prints_ref[...].reshape(slots * 8, width)
    for tile in range(TILES_DEV):
        sums = lax.dot_general(
            prints,
            cells_ref[:, tile * width : (tile + 1) * width],
            (((1,), (1,)), ((), ())),
            preferred_element_type=jnp.float32,
        )
        sums_ref[tile] = sums.reshape(slots, 8, 128)
    same = lax.rem(lax.broadcasted_iota(jnp.int32, (8, 128), 1), 8) == lax.broadcasted_iota(jnp.int32, (8, 128), 0)

    def pick(group, carry):
        at = pl.multiple_of(group * 8, 8)
        rows = [
            jnp.sum(jnp.where(same, sums_ref[loc_ref[at + i], at + i], 0.0), axis=0, keepdims=True) for i in range(8)
        ]
        out_ref[pl.ds(at, 8)] = jnp.concatenate(rows, axis=0)
        return carry

    lax.fori_loop(0, slots // 8, pick, 0, unroll=2)


def station_kernel(place_ref, count_ref, back_ref, out_ref, sums_ref):
    stations = sums_ref.shape[0]
    for station in range(stations):
        total = back_ref[pl.ds(place_ref[KT * station], 1)]
        for k in range(1, KT):
            row = back_ref[pl.ds(place_ref[KT * station + k], 1)]
            total = total + jnp.where(k < count_ref[station], row, 0.0)
        sums_ref[station : station + 1] = jnp.where(0 < count_ref[station], total, 0.0)
    lane = lax.broadcasted_iota(jnp.int32, (128, 16), 0)
    sample = lax.broadcasted_iota(jnp.int32, (128, 16), 1)
    fold = (lax.div(lane, 8) == sample).astype(jnp.float32)
    out_ref[...] = jnp.dot(
        sums_ref[...], fold, precision=lax.Precision.HIGHEST, preferred_element_type=jnp.float32
    )


def body(flux, coeff, diff_steps, footprint, tile_src, tile_local, tile_count):
    samples, rows, lon = flux.shape
    stations = footprint.shape[0]
    slots = stations * KT
    bands = lax.axis_size("station")
    band = lax.axis_index("station")
    part = lax.axis_index("sample")
    own = part.astype(jnp.int32).reshape(1)
    cells = rows * TILE_LON // PARTS
    down = [(i, i + 1) for i in range(bands - 1)]
    up = [(i + 1, i) for i in range(bands - 1)]

    above = lax.ppermute(flux[:, rows - HALO :], "station", down)
    below = lax.ppermute(flux[:, :HALO], "station", up)
    coef_above = lax.ppermute(coeff[rows - HALO :], "station", down)
    coef_below = lax.ppermute(coeff[:HALO], "station", up)

    src_all = tile_src.reshape(bands, slots)
    my_src = lax.dynamic_index_in_dim(src_all, band, 0, keepdims=False)
    prints = lax.dynamic_slice_in_dim(footprint, part * cells, cells, axis=2).reshape(slots, 8, TILE_LON)
    sent, place = pl.pallas_call(
        pack_kernel,
        out_shape=(
            jax.ShapeDtypeStruct((bands, 8 * CAP, TILE_LON), jnp.bfloat16),
            jax.ShapeDtypeStruct((slots,), jnp.int32),
        ),
        in_specs=[spec(SMEM), spec(VMEM)],
        out_specs=(spec(VMEM), spec(SMEM)),
        scratch_shapes=[SMEM((bands,), jnp.int32), SMEM((CAP * bands,), jnp.int32)],
        name="pack",
    )(my_src, prints)
    arrived = lax.all_to_all(sent, "station", split_axis=0, concat_axis=0, tiled=True)

    code = jnp.arange(slots, dtype=jnp.int32)[None, :] * 8 + tile_local.reshape(bands, slots)
    mine = src_all == band
    first = jnp.min(jnp.where(mine, code, slots * 8), axis=1)
    last = jnp.max(jnp.where(mine, code, 0), axis=1)
    loc = jnp.stack([first, last], axis=1).reshape(bands * CAP) & 7

    final = pl.pallas_call(
        diffuse_kernel,
        out_shape=jax.ShapeDtypeStruct((PARTS, samples * 8, lon), jnp.bfloat16),
        in_specs=[spec(SMEM), spec(SMEM)] + [spec(VMEM)] * 6,
        out_specs=spec(VMEM),
        scratch_shapes=[
            VMEM((2, 2, rows + 4 * HALO, lon), jnp.float32),
            VMEM((rows + 2 * HALO, lon), jnp.float32),
        ],
        compiler_params=pltpu.CompilerParams(vmem_limit_bytes=24 * 2**20),
        name="diffuse",
    )(own, diff_steps, flux, above, below, coeff, coef_above, coef_below)

    parts = [final[0]] + [
        lax.ppermute(final[turn], "sample", [(i, (i + turn) % PARTS) for i in range(PARTS)]) for turn in (3, 2, 1)
    ]

    values = pl.pallas_call(
        dots_kernel,
        out_shape=jax.ShapeDtypeStruct((bands * CAP, 128), jnp.float32),
        in_specs=[spec(SMEM), spec(SMEM)] + [spec(VMEM)] * 5,
        out_specs=spec(VMEM),
        scratch_shapes=[
            VMEM((samples * 8 * PARTS, lon), jnp.bfloat16),
            VMEM((TILES_DEV, bands * CAP, 8, 128), jnp.float32),
        ],
        compiler_params=pltpu.CompilerParams(vmem_limit_bytes=24 * 2**20),
        name="dots",
    )(own, loc, arrived, *parts)

    back = lax.all_to_all(values.reshape(bands, CAP, 128), "station", split_axis=0, concat_axis=0, tiled=True)
    share = pl.pallas_call(
        station_kernel,
        out_shape=jax.ShapeDtypeStruct((stations, 16), jnp.float32),
        in_specs=[spec(SMEM), spec(SMEM), spec(VMEM)],
        out_specs=spec(VMEM),
        scratch_shapes=[VMEM((stations, 128), jnp.float32)],
        name="stations",
    )(place, tile_count, back.reshape(bands * CAP, 128))
    others = [lax.ppermute(share, "sample", [(i, i ^ flip) for i in range(PARTS)]) for flip in (1, 2, 3)]
    return (share + others[0]) + (others[1] + others[2])


def solution(mesh):
    in_specs = (
        P("sample", "station", None),
        P("station", None),
        P("sample"),
        P("station", None, None),
        P(),
        P(),
        P("station"),
    )
    return jax.shard_map(body, mesh=mesh, in_specs=in_specs, out_specs=P("station", None), check_vma=False)
```

time: 552 us -> 115 us (0.21)
  waiting for transfers between devices: 343 us -> 11.6 us
  other arithmetic: 56.2 us -> 1.59 us
  local copies, waits for them, and re-layouts: 48.8 us -> 9.14 us
  starting transfers between devices: 64.6 us -> 31.8 us
  blocking collectives: 11 us -> 37.5 us
  matrix products: 25.6 us -> 0 us
  Pallas kernels: 0 us -> 21.5 us
    all_to_all x1, waiting for transfers between devices: 340 us -> 0.01 us  [body(): lax.all_to_all(sent, 'station', split_axis=0, concat_axis=0, tiled=True)]
    all_to_all x0 -> x1, blocking collectives: none -> 37.5 us  [body(): lax.all_to_all(values.reshape(bands, CAP, 128), 'station', split_axis=0,...]
    gather x4 -> x0, local copies, waits for them, and re-layouts: 30.8 us -> none  [the longest x1 17.1 us: body(): tiles[send_loc]]
    dot_general x3 -> x0, matrix products: 25.6 us -> none  [the longest x1 25.3 us: body(): jnp.einsum('ncst,nct->ncs', arrived, prints_laid, preferred_element_type=...]
    add x5 -> x1, other arithmetic: 24.3 us -> 1.3 us  [body(): return share + others[0] + (others[1] + others[2])]
    pallas_call x0 -> x4, Pallas kernels: none -> 21.5 us  [the longest x1 12.6 us: body(): pl.pallas_call(diffuse_kernel, out_shape=jax.ShapeDtypeStruct((PARTS, sam...]
    select_n x6 -> x0, other arithmetic: 19.9 us -> none  [the longest x1 12.1 us: body(): jnp.where(filled[:, :, None, None], tiles[send_loc], jnp.zeros((), jnp.bf...]
    ppermute x12 -> x10, starting transfers between devices: 37.7 us -> 19.9 us  [the longest x3 6.45 us: body(): lax.ppermute(final[turn], 'sample', [(i, (i + turn) % PARTS) for i in ran...]
  transfers between devices with their start and end apart: 13 -> 11, of which waited for: 6 -> 6; matrix products, arithmetic and copies ran while one was open for 6% -> 3% of each run, Pallas kernels for 0% -> 11%
where the time goes in v1:
time: 115 us; the launch traced here: 113 us
  blocking collectives  37.5 us (33%)
  starting transfers between devices  31.8 us (28%)
  Pallas kernels  21.5 us (19%)
  waiting for transfers between devices  11.6 us (10%)
  local copies, waits for them, and re-layouts  9.14 us (8%)
  other arithmetic  1.59 us (1%)
    all_to_all x1, blocking collectives, body(): lax.all_to_all(values.reshape(bands, CAP, 128), 'station', split_axis=0,...  37.5 us
    pallas_call x1, Pallas kernels, body(): pl.pallas_call(diffuse_kernel, out_shape=jax.ShapeDtypeStruct((PARTS, sam...  12.6 us
    all_to_all x1, starting transfers between devices, body(): lax.all_to_all(sent, 'station', split_axis=0, concat_axis=0, tiled=True)  11.9 us
    ppermute x3, waiting for transfers between devices, body(): lax.ppermute(final[turn], 'sample', [(i, (i + turn) % PARTS) for i in ran...  6.57 us
    ppermute x3, starting transfers between devices, body(): lax.ppermute(final[turn], 'sample', [(i, (i + turn) % PARTS) for i in ran...  6.45 us
    ppermute x3, starting transfers between devices, body(): lax.ppermute(share, 'sample', [(i, i ^ flip) for i in range(PARTS)])  4.7 us
    ppermute x1, starting transfers between devices, body(): coef_above = lax.ppermute(coeff[rows - HALO:], 'station', down)  4.16 us
    pallas_call x1, Pallas kernels, body(): pl.pallas_call(pack_kernel, out_shape=(jax.ShapeDtypeStruct((bands, 8 * C...  3.74 us
  transfers between devices with their start and end apart: 11, of which 6 were waited for; matrix products, arithmetic and copies ran while one was open for 3% of the time, Pallas kernels for 11%

profile of v1, /device:TPU:8, one launch (start us, length us, event | category | flops | bytes accessed | tf_op | source)
XLA Modules:
  0.0 113.3 jit_solution(2024271734940600274)
XLA Ops:
  0.0 0.0 copy-start
  0.0 1.1 copy.10
  1.1 0.3 reshape.41
  1.3 0.3 copy-done
  1.6 0.2 constant_dynamic-slice_fusion
  1.8 1.2 %reshape.42.prints_ref = bf16[64,8,512]{2,1,0:T(8,128)(2,1)} reshape(bf16[16,4,4096]{2,1,0:T(4,128)(2,1)S(1)} %constant_dynamic-slice_fusion) | data formatting | bytes 1048576 | tf_op jit(solution)/shard_map/reshape | solution.py:162
  3.0 0.0 copy-start.3
  3.0 0.5 dynamic-slice_bitcast_fusion.src_ref
  3.5 3.7 %pack.1 = (bf16[64,16,512]{2,1,0:T(8,128)(2,1)}, s32[64]{0:T(128)}) custom-call(s32[64]{0:T(128)} %dynamic-slice_bitcast_fusion.src_ref, bf16[64,8,512]{2,1,0:T(8,128)(2,1)} %reshape.42.prints_ref), custom_call_target="tpu_custom_call" | custom-call | tf_op jit(solution)/shard_map/pack/pallas_call | solution.py:163
  7.3 11.9 %all-to-all-start = ((bf16[64,16,512]{2,1,0:T(8,128)(2,1)}), bf16[64,16,512]{2,1,0:T(8,128)(2,1)S(1)}, u32[]{:S(2)}, u32[]{:S(2)}) async-start(bf16[64,16,512]{2,1,0:T(8,128)(2,1)} %get-tuple-element.8), calls=%async_computation | async-start | bytes 2097152 | tf_op jit(solution)/shard_map/all_to_all | solution.py:174
  19.2 1.1 fusion.2
  20.3 2.0 %collective-permute-start = (bf16[4,8,3584]{2,1,0:T(8,128)(2,1)S(1)}, bf16[4,8,3584]{2,1,0:T(8,128)(2,1)S(1)}, u32[]{:S(2)}, u32[]{:S(2)}) collective-permute-start(bf16[4,8,3584]{2,1,0:T(8,128)(2,1)S(1)} %get-tuple-element.16), channel_id=1, source_target_pairs={{0,4},{4,8},{8,12},{12,16},{16,20},{20,24},{24,28},{28,32},{32,36}... | collective-permute-start | bytes 688136 | tf_op jit(solution)/shard_map/ppermute | solution.py:155
  22.3 1.3 %collective-permute-start.1 = (bf16[4,8,3584]{2,1,0:T(8,128)(2,1)S(1)}, bf16[4,8,3584]{2,1,0:T(8,128)(2,1)S(1)}, u32[]{:S(2)}, u32[]{:S(2)}) collective-permute-start(bf16[4,8,3584]{2,1,0:T(8,128)(2,1)S(1)} %get-tuple-element.15), channel_id=1, source_target_pairs={{4,0},{8,4},{12,8},{16,12},{20,16},{24,20},{28,24},{32,28},{36,32}... | collective-permute-start | bytes 688136 | tf_op jit(solution)/shard_map/ppermute | solution.py:156
  23.6 1.0 fusion.3
  24.6 4.2 %collective-permute-start.2 = (f32[8,3584]{1,0:T(8,128)S(1)}, f32[8,3584]{1,0:T(8,128)S(1)}, u32[]{:S(2)}, u32[]{:S(2)}) collective-permute-start(f32[8,3584]{1,0:T(8,128)S(1)} %get-tuple-element.18), channel_id=1, source_target_pairs={{0,4},{4,8},{8,12},{12,16},{16,20},{20,24},{24,28},{28,32},{32,36}... | collective-permute-start | bytes 344072 | tf_op jit(solution)/shard_map/ppermute | solution.py:157
  28.7 1.3 %collective-permute-start.3 = (f32[8,3584]{1,0:T(8,128)S(1)}, f32[8,3584]{1,0:T(8,128)S(1)}, u32[]{:S(2)}, u32[]{:S(2)}) collective-permute-start(f32[8,3584]{1,0:T(8,128)S(1)} %get-tuple-element.17), channel_id=1, source_target_pairs={{4,0},{8,4},{12,8},{16,12},{20,16},{24,20},{28,24},{32,28},{36,32}... | collective-permute-start | bytes 344072 | tf_op jit(solution)/shard_map/ppermute | solution.py:158
  30.0 0.0 collective-permute-done.2.coef_above_ref
  30.1 3.1 %collective-permute-done.3.coef_below_ref = f32[8,3584]{1,0:T(8,128)S(1)} collective-permute-done((f32[8,3584]{1,0:T(8,128)S(1)}, f32[8,3584]{1,0:T(8,128)S(1)}, u32[]{:S(2)}, u32[]{:S(2)}) %collective-permute-start.3) | collective-permute-done | bytes 114720 | tf_op jit(solution)/shard_map/ppermute | solution.py:158
  33.2 0.0 collective-permute-done.above_ref
  33.2 0.0 collective-permute-done.1.below_ref
  33.2 0.0 copy-done.3
  33.2 0.0 copy-start.1
  33.2 1.2 %copy-done.1 = bf16[4,32,3584]{2,1,0:T(8,128)(2,1)S(1)} copy-done((bf16[4,32,3584]{2,1,0:T(8,128)(2,1)S(1)}, bf16[4,32,3584]{2,1,0:T(8,128)(2,1)}, u32[]{:S(2)}) %copy-start.1) | copy-done | bytes 917528
  34.4 0.0 copy-start.2
  34.4 1.0 copy-done.2
  35.4 0.0 copy-start.4
  35.4 0.0 copy-start.5
  35.4 12.6 %diffuse.1 = bf16[4,32,3584]{2,1,0:T(8,128)(2,1)S(1)} custom-call(s32[1]{0:T(128)} %bitcast.1.own_ref, s32[4]{0:T(128)S(1)} %copy-done.3, bf16[4,32,3584]{2,1,0:T(8,128)(2,1)S(1)} %copy-done.1, bf16[4,8,3584]{2,1,0:T(8,128)(2,1)S(1)} %collective-permute-done.above_ref, bf16[4,8,3584]{2,1,0:T(8,128)(2,1)S(1)} %collective-permute-done.1.below_ref, ...), custom_call_target="tpu_custom_call" | custom-call | tf_op jit(solution)/shard_map/diffuse/pallas_call | solution.py:182
  48.0 0.9 slice_bitcast_fusion
  48.9 0.0 collective-permute-start.4
  48.9 6.4 %collective-permute-start.5 = (bf16[32,3584]{1,0:T(8,128)(2,1)}, bf16[32,3584]{1,0:T(8,128)(2,1)}, u32[]{:S(2)}, u32[]{:S(2)}) collective-permute-start(bf16[32,3584]{1,0:T(8,128)(2,1)} %get-tuple-element.12), channel_id=1, source_target_pairs={{0,2},{1,3},{2,0},{3,1},{4,6},{5,7},{6,4},{7,5},{8,10},{9,11},{10,... | collective-permute-start | bytes 688136 | tf_op jit(solution)/shard_map/ppermute | solution.py:196
  55.3 0.0 collective-permute-start.6
  55.3 0.1 add.35
  55.4 0.0 copy-done.4
  55.4 0.0 copy-done.5
  55.5 0.1 reduce_max.14
  55.6 0.1 reduce_min.14
  55.6 0.1 reduce_max.18
  55.8 0.1 reduce_min.18
  55.9 0.1 copy.12
  56.0 0.1 and.12.loc_ref
  56.1 2.0 %collective-permute-done.4.part1 = bf16[32,3584]{1,0:T(8,128)(2,1)} collective-permute-done((bf16[32,3584]{1,0:T(8,128)(2,1)}, bf16[32,3584]{1,0:T(8,128)(2,1)}, u32[]{:S(2)}, u32[]{:S(2)}) %collective-permute-start.4) | collective-permute-done | bytes 229408 | tf_op jit(solution)/shard_map/ppermute | solution.py:196
  58.1 3.9 %collective-permute-done.5.part2 = bf16[32,3584]{1,0:T(8,128)(2,1)} collective-permute-done((bf16[32,3584]{1,0:T(8,128)(2,1)}, bf16[32,3584]{1,0:T(8,128)(2,1)}, u32[]{:S(2)}, u32[]{:S(2)}) %collective-permute-start.5) | collective-permute-done | bytes 229408 | tf_op jit(solution)/shard_map/ppermute | solution.py:196
  62.1 0.7 collective-permute-done.6.part3
  62.7 0.0 all-to-all-done.prints_ref
  62.7 3.5 %dots.1 = f32[128,128]{1,0:T(8,128)S(1)} custom-call(s32[1]{0:T(128)} %bitcast.1.own_ref, s32[128]{0:T(128)S(1)} %and.12.loc_ref, bf16[64,16,512]{2,1,0:T(8,128)(2,1)S(1)} %all-to-all-done.prints_ref, bf16[32,3584]{1,0:T(8,128)(2,1)S(1)} %get-tuple-element.14.own_part, bf16[32,3584]{1,0:T(8,128)(2,1)} %collective-permute-done.4.part1, ...), custom_call_target="tpu_custom_call" | custom-call | tf_op jit(solution)/shard_map/dots/pallas_call | solution.py:199
  66.2 37.5 %all_to_all.10 = f32[64,2,128]{2,1,0:T(2,128)} all-to-all(f32[64,2,128]{2,1,0:T(2,128)S(1)} %bitcast.26), channel_id=1, replica_groups=mesh['station'=64,'sample'=4] {'station'}, dimensions={0} | all-to-all | bytes 131072 | tf_op jit(solution)/shard_map/all_to_all | solution.py:212
  103.8 1.7 %stations.1 = f32[16,16]{1,0:T(8,128)} custom-call(s32[64]{0:T(128)} %get-tuple-element.7.place_ref, s32[16]{0:T(128)} %count_ref.1, f32[128,128]{1,0:T(8,128)} %bitcast.27), custom_call_target="tpu_custom_call" | custom-call | tf_op jit(solution)/shard_map/stations/pallas_call | solution.py:213
  105.5 0.0 collective-permute-start.8
  105.5 1.8 %collective-permute-start.9 = (f32[16,16]{1,0:T(8,128)}, f32[16,16]{1,0:T(8,128)S(1)}, u32[]{:S(2)}, u32[]{:S(2)}) collective-permute-start(f32[16,16]{1,0:T(8,128)} %stations.1), channel_id=1, source_target_pairs={{0,3},{1,2},{2,1},{3,0},{4,7},{5,6},{6,5},{7,4},{8,11},{9,10},{10,... | collective-permute-start | bytes 3080 | tf_op jit(solution)/shard_map/ppermute | solution.py:221
  107.2 2.9 %collective-permute-start.7 = (f32[16,16]{1,0:T(8,128)}, f32[16,16]{1,0:T(8,128)S(1)}, u32[]{:S(2)}, u32[]{:S(2)}) collective-permute-start(f32[16,16]{1,0:T(8,128)} %stations.1), channel_id=1, source_target_pairs={{0,1},{1,0},{2,3},{3,2},{4,5},{5,4},{6,7},{7,6},{8,9},{9,8},{10,11... | collective-permute-start | bytes 3080 | tf_op jit(solution)/shard_map/ppermute | solution.py:221
  110.2 0.7 collective-permute-done.8
  110.8 0.0 collective-permute-done.9
  110.8 1.2 %collective-permute-done.7 = f32[16,16]{1,0:T(8,128)S(1)} collective-permute-done((f32[16,16]{1,0:T(8,128)}, f32[16,16]{1,0:T(8,128)S(1)}, u32[]{:S(2)}, u32[]{:S(2)}) %collective-permute-start.7) | collective-permute-done | bytes 1056 | tf_op jit(solution)/shard_map/ppermute | solution.py:221
  112.0 1.3 %add_add_fusion = f32[16,16]{1,0:T(8,128)} fusion(f32[16,16]{1,0:T(8,128)S(1)} %collective-permute-done.8, f32[16,16]{1,0:T(8,128)S(1)} %collective-permute-done.9, f32[16,16]{1,0:T(8,128)} %stations.1, f32[16,16]{1,0:T(8,128)S(1)} %collective-permute-done.7), kind=kLoop, calls=%fused_computation.9 | loop fusion | flops 768 | bytes 5120 | tf_op jit(solution)/shard_map/add | solution.py:222
  (4 shorter events, 0.1 us)
Async XLA Ops:
  0.0 1.6 %copy-start = (bf16[16,4,16384]{2,1,0:T(4,128)(2,1)S(1)}, bf16[16,4,16384]{2,1,0:T(4,128)(2,1)}, u32[]{:S(2)}) copy-start(bf16[16,4,16384]{2,1,0:T(4,128)(2,1)} %param.10) | copy-start | bytes 6291460
  3.0 30.2 %copy-start.3 = (s32[4]{0:T(128)S(1)}, s32[4]{0:T(128)}, u32[]{:S(2)}) copy-start(s32[4]{0:T(128)} %steps_ref.1) | copy-start | bytes 52
  7.3 55.4 %all-to-all-start = ((bf16[64,16,512]{2,1,0:T(8,128)(2,1)}), bf16[64,16,512]{2,1,0:T(8,128)(2,1)S(1)}, u32[]{:S(2)}, u32[]{:S(2)}) async-start(bf16[64,16,512]{2,1,0:T(8,128)(2,1)} %get-tuple-element.8), calls=%async_computation | async-start | bytes 2097152 | tf_op jit(solution)/shard_map/all_to_all | solution.py:174
  20.3 12.9 %collective-permute-start = (bf16[4,8,3584]{2,1,0:T(8,128)(2,1)S(1)}, bf16[4,8,3584]{2,1,0:T(8,128)(2,1)S(1)}, u32[]{:S(2)}, u32[]{:S(2)}) collective-permute-start(bf16[4,8,3584]{2,1,0:T(8,128)(2,1)S(1)} %get-tuple-element.16), channel_id=1, source_target_pairs={{0,4},{4,8},{8,12},{12,16},{16,20},{20,24},{24,28},{28,32},{32,36}... | collective-permute-start | bytes 688136 | tf_op jit(solution)/shard_map/ppermute | solution.py:155
  22.3 10.9 %collective-permute-start.1 = (bf16[4,8,3584]{2,1,0:T(8,128)(2,1)S(1)}, bf16[4,8,3584]{2,1,0:T(8,128)(2,1)S(1)}, u32[]{:S(2)}, u32[]{:S(2)}) collective-permute-start(bf16[4,8,3584]{2,1,0:T(8,128)(2,1)S(1)} %get-tuple-element.15), channel_id=1, source_target_pairs={{4,0},{8,4},{12,8},{16,12},{20,16},{24,20},{28,24},{32,28},{36,32}... | collective-permute-start | bytes 688136 | tf_op jit(solution)/shard_map/ppermute | solution.py:156
  24.6 5.5 %collective-permute-start.2 = (f32[8,3584]{1,0:T(8,128)S(1)}, f32[8,3584]{1,0:T(8,128)S(1)}, u32[]{:S(2)}, u32[]{:S(2)}) collective-permute-start(f32[8,3584]{1,0:T(8,128)S(1)} %get-tuple-element.18), channel_id=1, source_target_pairs={{0,4},{4,8},{8,12},{12,16},{16,20},{20,24},{24,28},{28,32},{32,36}... | collective-permute-start | bytes 344072 | tf_op jit(solution)/shard_map/ppermute | solution.py:157
  28.7 4.5 %collective-permute-start.3 = (f32[8,3584]{1,0:T(8,128)S(1)}, f32[8,3584]{1,0:T(8,128)S(1)}, u32[]{:S(2)}, u32[]{:S(2)}) collective-permute-start(f32[8,3584]{1,0:T(8,128)S(1)} %get-tuple-element.17), channel_id=1, source_target_pairs={{4,0},{8,4},{12,8},{16,12},{20,16},{24,20},{28,24},{32,28},{36,32}... | collective-permute-start | bytes 344072 | tf_op jit(solution)/shard_map/ppermute | solution.py:158
  33.2 1.2 %copy-start.1 = (bf16[4,32,3584]{2,1,0:T(8,128)(2,1)S(1)}, bf16[4,32,3584]{2,1,0:T(8,128)(2,1)}, u32[]{:S(2)}) copy-start(bf16[4,32,3584]{2,1,0:T(8,128)(2,1)} %flux_ref.1) | copy-start | bytes 2752516
  34.4 1.0 copy-start.2
  35.4 20.0 %copy-start.4 = (s32[1024,4,1]{0,2,1:T(1,128)S(1)}, s32[1024,4,1]{0,2,1:T(1,128)}, u32[]{:S(2)}) copy-start(s32[1024,4,1]{0,2,1:T(1,128)} %param.11) | copy-start | bytes 49156
  35.4 20.0 %copy-start.5 = (s32[1024,4]{0,1:T(4,128)S(1)}, s32[1024,4]{0,1:T(4,128)}, u32[]{:S(2)}) copy-start(s32[1024,4]{0,1:T(4,128)} %param.12) | copy-start | bytes 49156
  48.9 9.3 %collective-permute-start.4 = (bf16[32,3584]{1,0:T(8,128)(2,1)}, bf16[32,3584]{1,0:T(8,128)(2,1)}, u32[]{:S(2)}, u32[]{:S(2)}) collective-permute-start(bf16[32,3584]{1,0:T(8,128)(2,1)} %get-tuple-element.13), channel_id=1, source_target_pairs={{0,3},{1,0},{2,1},{3,2},{4,7},{5,4},{6,5},{7,6},{8,11},{9,8},{10,9... | collective-permute-start | bytes 688136 | tf_op jit(solution)/shard_map/ppermute | solution.py:196
  48.9 13.2 %collective-permute-start.5 = (bf16[32,3584]{1,0:T(8,128)(2,1)}, bf16[32,3584]{1,0:T(8,128)(2,1)}, u32[]{:S(2)}, u32[]{:S(2)}) collective-permute-start(bf16[32,3584]{1,0:T(8,128)(2,1)} %get-tuple-element.12), channel_id=1, source_target_pairs={{0,2},{1,3},{2,0},{3,1},{4,6},{5,7},{6,4},{7,5},{8,10},{9,11},{10,... | collective-permute-start | bytes 688136 | tf_op jit(solution)/shard_map/ppermute | solution.py:196
  55.3 7.4 %collective-permute-start.6 = (bf16[32,3584]{1,0:T(8,128)(2,1)}, bf16[32,3584]{1,0:T(8,128)(2,1)}, u32[]{:S(2)}, u32[]{:S(2)}) collective-permute-start(bf16[32,3584]{1,0:T(8,128)(2,1)} %get-tuple-element.11), channel_id=1, source_target_pairs={{0,1},{1,2},{2,3},{3,0},{4,5},{5,6},{6,7},{7,4},{8,9},{9,10},{10,1... | collective-permute-start | bytes 688136 | tf_op jit(solution)/shard_map/ppermute | solution.py:196
  105.5 5.4 %collective-permute-start.8 = (f32[16,16]{1,0:T(8,128)}, f32[16,16]{1,0:T(8,128)S(1)}, u32[]{:S(2)}, u32[]{:S(2)}) collective-permute-start(f32[16,16]{1,0:T(8,128)} %stations.1), channel_id=1, source_target_pairs={{0,2},{1,3},{2,0},{3,1},{4,6},{5,7},{6,4},{7,5},{8,10},{9,11},{10,... | collective-permute-start | bytes 3080 | tf_op jit(solution)/shard_map/ppermute | solution.py:221
  105.5 5.4 %collective-permute-start.9 = (f32[16,16]{1,0:T(8,128)}, f32[16,16]{1,0:T(8,128)S(1)}, u32[]{:S(2)}, u32[]{:S(2)}) collective-permute-start(f32[16,16]{1,0:T(8,128)} %stations.1), channel_id=1, source_target_pairs={{0,3},{1,2},{2,1},{3,0},{4,7},{5,6},{6,5},{7,4},{8,11},{9,10},{10,... | collective-permute-start | bytes 3080 | tf_op jit(solution)/shard_map/ppermute | solution.py:221
  107.2 4.8 %collective-permute-start.7 = (f32[16,16]{1,0:T(8,128)}, f32[16,16]{1,0:T(8,128)S(1)}, u32[]{:S(2)}, u32[]{:S(2)}) collective-permute-start(f32[16,16]{1,0:T(8,128)} %stations.1), channel_id=1, source_target_pairs={{0,1},{1,0},{2,3},{3,2},{4,5},{5,4},{6,7},{7,6},{8,9},{9,8},{10,11... | collective-permute-start | bytes 3080 | tf_op jit(solution)/shard_map/ppermute | solution.py:221
